TPU v7x, 32 devices: a whole 2x2x4 slice. The times are simulated.
32 devices in a mesh: rep: 2 (over x), fsdp: 16 (over z, y, core).
Axes of the slice: x: 2, y: 2, z: 4, core: 2. Of those that a mesh axis runs over, the one named last changes fastest.
Arguments:
- activations: bfloat16 [2, 2, 2816, 2560], P('rep', None, 'fsdp'), may hold values from -6 to 6
- residual: bfloat16 [2, 2, 2816, 5120], P('rep', None, 'fsdp'), may hold values from -6 to 6
- upstream: bfloat16 [2, 2, 2816, 5120], P('rep', None, 'fsdp'), may hold values from -6 to 6
- norm_gain: float32 [5120], replicated, may hold values from 0.5 to 1.5
- params: float32 [2, 128, 40, 5, 128], P('rep', 'fsdp'), may hold values from -6 to 6
- momentum: float32 [2, 128, 40, 5, 128], P('rep', 'fsdp'), may hold values from -6 to 6
- pattern: int32 [40, 5], replicated, may hold values from 0 to 19, as said below
- step_index: int32 [1], replicated, may hold values from 0 to 2999
Outputs:
- params_out: float32 [2, 128, 40, 5, 128], P('rep', 'fsdp')
- momentum_out: float32 [2, 128, 40, 5, 128], P('rep', 'fsdp')
Inputs may be any that keep to these rules, and one draw needn't show every extreme that they name: `pattern`: each output block column c lists 5 different input blocks, the first of them c mod 20.
All inputs are finite; a program needn't handle non-finite values.
Results may differ from a plain program's by a relative error of at most 0.012.
Values may be sent and summed in bfloat16 or wider, within the bound.
No kernel may reach another device: no remote copies, remote signals or barrier semaphores. Data moves between devices by JAX's collectives and lax.ppermute only.
A program may use at most 128 MiB of HBM per device.

v0:
```python
from functools import partial
import math

import jax
import jax.numpy as jnp
from jax import lax
from jax.sharding import PartitionSpec as P

learn_rate = 0.1
momentum_beta = 0.9
decay_keep = 0.999
epsilon = 1e-06


def as_sent(array):
    return jax.tree.map(lambda a: a.astype(jnp.bfloat16) if a.dtype == jnp.float32 else a, array)


def shifted(array, axis, by):
    devices = lax.axis_size(axis)
    return lax.ppermute(array, axis, [(i, (i + by) % devices) for i in range(devices)])


def norm_backward(pre_norm, upstream_rows, gain):
    inv_rms = lax.rsqrt(jnp.mean(pre_norm * pre_norm, axis=-1, keepdims=True) + epsilon)
    weighted = gain * upstream_rows
    inner_mean = jnp.mean(pre_norm * weighted, axis=-1, keepdims=True)
    return inv_rms * weighted - pre_norm * inv_rms * inv_rms * inv_rms * inner_mean


def gossip(weights, stride):
    stride = stride % lax.axis_size("rep")
    if stride == 0:
        return weights
    partner = jax.tree.map(
        lambda part, own: part.astype(own.dtype), shifted(as_sent(weights), "rep", stride), weights
    )
    return 0.5 * (weights + partner)


def body(activations, residual, upstream, norm_gain, params, momentum, pattern, step_index):
    block_size = params.shape[4]
    per_col = pattern.shape[1]
    out_blocks = pattern.shape[0]
    scaling = 1.0 / math.sqrt(per_col * block_size)
    tok_rows = activations.shape[2]
    model_width = residual.shape[3]
    in_blocks = activations.shape[3] // block_size
    weights_now = params
    moment = momentum
    for step_num in range(activations.shape[1]):
        blocks = activations[0, step_num].reshape(tok_rows, in_blocks, block_size)
        picked = jnp.take(blocks, pattern, axis=1)
        low_weights = weights_now[0].astype(jnp.bfloat16)
        gathered = lax.all_gather(low_weights, "fsdp", axis=0, tiled=True)
        summed = jnp.einsum("tcki,icko->tco", picked, gathered, preferred_element_type=jnp.float32)
        pre_norm = residual[0, step_num].astype(jnp.float32) + scaling * summed.reshape(
            tok_rows, model_width
        )
        grad_pre = norm_backward(pre_norm, upstream[0, step_num].astype(jnp.float32), norm_gain)
        grad_low = grad_pre.astype(jnp.bfloat16).reshape(tok_rows, out_blocks, block_size)
        partial_sum = jnp.einsum(
            "tcki,tco->icko", picked, grad_low, preferred_element_type=jnp.float32
        )
        gradient = lax.psum_scatter(
            partial_sum.astype(jnp.bfloat16), "fsdp", scatter_dimension=0, tiled=True
        ).astype(jnp.float32)
        moment = momentum_beta * moment + (scaling * gradient)[None]
        weights_now = decay_keep * weights_now - learn_rate * moment
        branches = [partial(gossip, stride=1), partial(gossip, stride=2), partial(gossip, stride=4)]
        weights_now = lax.switch((step_index[0] + step_num) % 3, branches, weights_now)
    return (weights_now, moment)


def solution(mesh):
    in_specs = (
        P("rep", None, "fsdp", None),
        P("rep", None, "fsdp", None),
        P("rep", None, "fsdp", None),
        P(),
        P("rep", "fsdp", None, None, None),
        P("rep", "fsdp", None, None, None),
        P(),
        P(),
    )
    out_specs = (P("rep", "fsdp", None, None, None), P("rep", "fsdp", None, None, None))
    return jax.shard_map(body, mesh=mesh, in_specs=in_specs, out_specs=out_specs, check_vma=False)
```

profile of v0, /device:TPU:0, one launch (start us, length us, event | category | flops | bytes accessed | tf_op | source)
XLA Modules:
  0.0 411.8 jit_solution(7872160332571967769)
XLA Ops:
  7.2 2.1 copy.123
  9.4 2.5 fusion.67
  12.9 4.4 %convert_bitcast_fusion.1 = (f32[22,8,40,128]{3,1,2,0:T(8,128)}, f32[22,8,40,128]{3,1,2,0:T(8,128)S(1)}) fusion(bf16[1,2,176,5120]{3,2,1,0:T(8,128)(2,1)} %param.18), kind=kLoop, calls=%fused_computation.29 | loop fusion | flops 1802240 | bytes 10813440
  17.3 2.5 copy.82
  20.4 2.4 convert_bitcast_fusion.2
  22.7 2.5 copy.83
  25.3 9.7 %gather_fusion = bf16[200,176,128]{2,1,0:T(8,128)(2,1)} fusion(bf16[176,20,128]{2,0,1:T(8,128)(2,1)S(1)} %copy.62, s32[1024]{0:T(1024)S(1)} %pad_clamp_fusion), kind=kCustom, calls=%fused_computation.clone | custom fusion | bytes 18023200 | tf_op jit(solution)/shard_map/jit(_take)/gather | solution.py:53
  34.9 45.8 %all-gather.5.cloned.1.call-done = bf16[1,128,40,5,128]{4,1,3,2,0:T(8,128)(2,1)} async-done(((bf16[1,8,40,5,128]{4,1,3,2,0:T(8,128)(2,1)}), bf16[1,128,40,5,128]{4,1,3,2,0:T(8,128)(2,1)}) %all-gather.5.cloned.1.call-update) | async-done | bytes 6553616 | tf_op jit(solution)/shard_map/all_gather | solution.py:55
  80.7 10.4 %fusion.7 = f32[40,176,128,1]{2,1,3,0:T(8,128)} fusion(bf16[40,5,176,128]{3,2,1,0:T(8,128)(2,1)} %bitcast.185, pred[40,5]{1,0:T(8,128)(4,1)S(1)} %copy.60, bf16[1,128,40,5,128]{4,1,3,2,0:T(8,128)(2,1)} %all-gather.5.cloned.1.call-done), kind=kOutput, calls=%fused_computation.14 | convolution fusion | flops 1157939200 | bytes 19169480 | tf_op jit(solution)/shard_map/tcki,icko->tco/dot_general | solution.py:56
  91.1 3.8 multiply_reduce_fusion.1
  94.9 15.0 %fusion.20 = bf16[128,40,5,128]{0,3,2,1:T(8,128)(2,1)} fusion(bf16[40,5,176,128]{3,2,1,0:T(8,128)(2,1)S(1)} %bitcast.186, pred[40,5]{1,0:T(8,128)(4,1)S(1)} %copy.60, f32[176,40,128]{2,1,0:T(8,128)} %bitcast.188, f32[176,40,128]{2,1,0:T(8,128)} %bitcast.187, f32[40,176,128,1]{2,1,3,0:T(8,128)} %fusion.7, f32[176]{0:T(256)S(1)} %get-tuple-element.91, ...), kind=kOutput, calls=%fused_computation.23 | convolution fusion | flops 1170227200 | bytes 26400328 | tf_op jit(solution)/shard_map/tcki,tco->icko/dot_general | solution.py:62
  109.9 10.7 %copy.67 = bf16[128,40,5,128]{3,1,2,0:T(8,128)(2,1)} copy(bf16[128,40,5,128]{0,3,2,1:T(8,128)(2,1)} %fusion.20) | data formatting | bytes 13107200 | tf_op jit(solution)/shard_map/convert_element_type | solution.py:66
  121.5 84.5 %reduce-scatter.3.cloned.1.call-done = bf16[8,40,5,128]{3,1,2,0:T(8,128)(2,1)} async-done(((bf16[128,40,5,128]{3,1,2,0:T(8,128)(2,1)}), bf16[8,40,5,128]{3,1,2,0:T(8,128)(2,1)}) %reduce-scatter.3.cloned.1.call-update) | async-done | bytes 409616 | tf_op jit(solution)/shard_map/reduce_scatter | solution.py:65
  208.9 9.6 %gather_fusion.1 = bf16[200,176,128]{2,1,0:T(8,128)(2,1)} fusion(bf16[176,20,128]{2,0,1:T(8,128)(2,1)S(1)} %copy.71, s32[1024]{0:T(1024)S(1)} %pad_clamp_fusion), kind=kCustom, calls=%fused_computation.1.clone | custom fusion | bytes 18023200 | tf_op jit(solution)/shard_map/jit(_take)/gather | solution.py:53
  218.5 4.7 %copy.84 = f32[22,8,40,128]{3,2,1,0:T(8,128)} copy(f32[22,8,40,128]{3,1,2,0:T(8,128)} %get-tuple-element.84) | data formatting | bytes 7208960
  223.2 2.4 copy.85
  225.6 49.6 %all-gather.7.cloned.1.call-done = bf16[1,128,40,5,128]{4,1,3,2,0:T(8,128)(2,1)} async-done(((bf16[1,8,40,5,128]{4,1,3,2,0:T(8,128)(2,1)}), bf16[1,128,40,5,128]{4,1,3,2,0:T(8,128)(2,1)}) %all-gather.7.cloned.1.call-update) | async-done | bytes 6553616 | tf_op jit(solution)/shard_map/all_gather | solution.py:55
  275.3 10.5 %fusion.3 = f32[40,128,176,1]{1,2,3,0:T(8,128)} fusion(bf16[40,5,176,128]{3,2,1,0:T(8,128)(2,1)} %bitcast.181, pred[40,5]{1,0:T(8,128)(4,1)S(1)} %copy.60, bf16[1,128,40,5,128]{4,1,3,2,0:T(8,128)(2,1)} %all-gather.7.cloned.1.call-done), kind=kOutput, calls=%fused_computation.10 | convolution fusion | flops 1157939200 | bytes 19169480 | tf_op jit(solution)/shard_map/tcki,icko->tco/dot_general | solution.py:56
  285.7 3.8 multiply_reduce_fusion
  289.6 15.3 %fusion.17 = bf16[128,40,5,128]{0,3,2,1:T(8,128)(2,1)} fusion(bf16[40,5,176,128]{3,2,1,0:T(8,128)(2,1)S(1)} %bitcast.184, pred[40,5]{1,0:T(8,128)(4,1)S(1)} %copy.60, f32[176,40,128]{2,1,0:T(8,128)} %bitcast.190, f32[176,40,128]{2,1,0:T(8,128)} %bitcast.189, f32[40,128,176,1]{1,2,3,0:T(8,128)} %fusion.3, f32[176]{0:T(256)S(1)} %broadcast_multiply_fusion, ...), kind=kOutput, calls=%fused_computation.22 | convolution fusion | flops 1170227200 | bytes 26400328 | tf_op jit(solution)/shard_map/tcki,tco->icko/dot_general | solution.py:62
  304.8 10.7 %copy.75 = bf16[128,40,5,128]{3,1,2,0:T(8,128)(2,1)} copy(bf16[128,40,5,128]{0,3,2,1:T(8,128)(2,1)} %fusion.17) | data formatting | bytes 13107200 | tf_op jit(solution)/shard_map/convert_element_type | solution.py:66
  315.6 85.2 %reduce-scatter.5.cloned.1.call-done = bf16[8,40,5,128]{3,1,2,0:T(8,128)(2,1)} async-done(((bf16[128,40,5,128]{3,1,2,0:T(8,128)(2,1)}), bf16[8,40,5,128]{3,1,2,0:T(8,128)(2,1)}) %reduce-scatter.5.cloned.1.call-update) | async-done | bytes 409616 | tf_op jit(solution)/shard_map/reduce_scatter | solution.py:65
  400.8 2.1 bitcast_add_fusion.2
  403.0 1.3 conditional.3
  (59 shorter events, 6.9 us)
Async XLA Ops:
  7.2 73.6 %all-gather.5.cloned.1.call-start = ((), (), s32[]{:S(2)}) async-start(), calls=%async_computation.4 | async-start | bytes 6963200 | tf_op jit(solution)/shard_map/all_gather | solution.py:55
  9.3 3.2 copy-start.12
  9.3 196.7 %reduce-scatter.3.cloned.1.call-start = ((), (), s32[]{:S(2)}) async-start(), calls=%async_computation.2 | async-start | bytes 6963200 | tf_op jit(solution)/shard_map/reduce_scatter | solution.py:65
  17.3 3.1 copy-start.2
  80.7 10.4 %copy-start.3 = (bf16[1,2,176,5120]{3,2,1,0:T(8,128)(2,1)S(1)}, bf16[1,2,176,5120]{3,2,1,0:T(8,128)(2,1)}, u32[]{:S(2)}) copy-start(bf16[1,2,176,5120]{3,2,1,0:T(8,128)(2,1)} %param.17) | copy-start | bytes 10813444
  80.7 10.4 %copy-start.11 = (f32[5120]{0:T(1024)S(1)}, f32[5120]{0:T(1024)}, u32[]{:S(2)}) copy-start(f32[5120]{0:T(1024)} %param.19) | copy-start | bytes 61444
  80.7 14.2 %copy-start = (bf16[200,176,128]{2,1,0:T(8,128)(2,1)S(1)}, bf16[200,176,128]{2,1,0:T(8,128)(2,1)}, u32[]{:S(2)}) copy-start(bf16[200,176,128]{2,1,0:T(8,128)(2,1)} %gather_fusion) | copy-start | bytes 27033604
  120.7 85.3 %copy-start.6 = (f32[1,8,40,5,128]{4,2,3,1,0:T(8,128)S(1)}, f32[1,8,40,5,128]{4,2,3,1,0:T(8,128)}, u32[]{:S(2)}) copy-start(f32[1,8,40,5,128]{4,2,3,1,0:T(8,128)} %param.20) | copy-start | bytes 2457604
  120.7 85.3 %copy-start.7 = (f32[1,8,40,5,128]{4,2,3,1,0:T(8,128)S(1)}, f32[1,8,40,5,128]{4,2,3,1,0:T(8,128)}, u32[]{:S(2)}) copy-start(f32[1,8,40,5,128]{4,2,3,1,0:T(8,128)} %param.21) | copy-start | bytes 2457604
  120.7 154.6 %all-gather.7.cloned.1.call-start = ((), (), s32[]{:S(2)}) async-start(), calls=%async_computation.5 | async-start | bytes 6963200 | tf_op jit(solution)/shard_map/all_gather | solution.py:55
  121.5 86.7 %copy-start.5 = (bf16[1,1,176,2560]{3,2,1,0:T(8,128)(2,1)S(1)}, bf16[1,1,176,2560]{3,2,1,0:T(8,128)(2,1)}, u32[]{:S(2)}) copy-start(bf16[1,1,176,2560]{3,2,1,0:T(8,128)(2,1)} %get-tuple-element.88) | copy-start | bytes 2703364
  208.2 192.6 %reduce-scatter.5.cloned.1.call-start = ((), (), s32[]{:S(2)}) async-start(), calls=%async_computation.3 | async-start | bytes 6963200 | tf_op jit(solution)/shard_map/reduce_scatter | solution.py:65
  218.5 4.7 %copy-start.1 = (f32[22,8,40,128]{3,1,2,0:T(8,128)S(1)}, f32[22,8,40,128]{3,1,2,0:T(8,128)}, u32[]{:S(2)}) copy-start(f32[22,8,40,128]{3,1,2,0:T(8,128)} %get-tuple-element.86) | copy-start | bytes 10813444
  223.2 66.3 %slice-start = ((s8[9011200]{0:T(1024)(128)(4,1)}), s8[622592]{0:T(1024)(128)(4,1)S(1)}, s32[]{:S(2)}) async-start(s8[9011200]{0:T(1024)(128)(4,1)} %bitcast.182), calls=%async_computation.6 | async-start | bytes 1245184
  275.2 10.5 %copy-start.4 = (bf16[1,2,176,5120]{3,2,1,0:T(8,128)(2,1)S(1)}, bf16[1,2,176,5120]{3,2,1,0:T(8,128)(2,1)}, u32[]{:S(2)}) copy-start(bf16[1,2,176,5120]{3,2,1,0:T(8,128)(2,1)} %param.17) | copy-start | bytes 10813444
  275.2 14.3 %slice-start.1 = ((s8[9011200]{0:T(1024)(128)(4,1)}), s8[4194304]{0:T(1024)(128)(4,1)S(1)}, s32[]{:S(2)}) async-start(s8[9011200]{0:T(1024)(128)(4,1)} %bitcast.182), calls=%async_computation.7 | async-start | bytes 8388608
  275.3 14.3 %slice-start.2 = ((s8[9011200]{0:T(1024)(128)(4,1)}), s8[4194304]{0:T(1024)(128)(4,1)S(1)}, s32[]{:S(2)}) async-start(s8[9011200]{0:T(1024)(128)(4,1)} %bitcast.182), calls=%async_computation.8 | async-start | bytes 8388608
  315.6 85.3 %copy-start.8 = (f32[1,8,40,5,128]{4,2,3,1,0:T(8,128)S(1)}, f32[1,8,40,5,128]{4,2,3,1,0:T(8,128)}, u32[]{:S(2)}) copy-start(f32[1,8,40,5,128]{4,2,3,1,0:T(8,128)} %param.21) | copy-start | bytes 2457604
  315.6 85.3 %copy-start.9 = (bf16[8,40,5,128]{3,1,2,0:T(8,128)(2,1)S(1)}, bf16[8,40,5,128]{3,1,2,0:T(8,128)(2,1)}, u32[]{:S(2)}) copy-start(bf16[8,40,5,128]{3,1,2,0:T(8,128)(2,1)} %reduce-scatter.3.cloned.1.call-done) | copy-start | bytes 1228804
  404.3 0.9 copy-start.10
Sparse Core Ops, SparseCore 0:
  10.7 69.9 all-gather.4
  120.8 85.1 reduce-scatter.2
  209.0 66.2 all-gather.6
  315.7 85.0 reduce-scatter.4
where the time goes:
time: 413 us; the launch traced here: 412 us
  waiting for transfers between devices  265 us (64%)
  local copies, waits for them, and re-layouts  61.5 us (15%)
  matrix products  51.2 us (12%)
  other arithmetic  19 us (5%)
  between operations  14.7 us (4%)
    reduce_scatter x2, waiting for transfers between devices, body(): lax.psum_scatter(partial_sum.astype(jnp.bfloat16), 'fsdp', scatter_dimens...  170 us
    all_gather x2, waiting for transfers between devices, body(): gathered = lax.all_gather(low_weights, 'fsdp', axis=0, tiled=True)  95.4 us
    dot_general x2, matrix products, body(): jnp.einsum('tcki,tco->icko', picked, grad_low, preferred_element_type=jnp...  30.3 us
    convert_element_type x2, local copies, waits for them, and re-layouts, body(): partial_sum.astype(jnp.bfloat16)  21.4 us
    dot_general x2, matrix products, body(): jnp.einsum('tcki,icko->tco', picked, gathered, preferred_element_type=jnp...  20.8 us
    gather x2, local copies, waits for them, and re-layouts, body(): picked = jnp.take(blocks, pattern, axis=1)  19.3 us
    unnamed x37, local copies, waits for them, and re-layouts  15.7 us
  transfers between devices with their start and end apart: 4, of which 4 were waited for; matrix products, arithmetic and copies ran while one was open for 10% of the time, Pallas kernels for 0%

commit v1 on v0

v1 whole, which is shorter than its diff:
```python
import math
from functools import partial

import jax
import jax.numpy as jnp
from jax import lax
from jax.experimental import pallas as pl
from jax.experimental.pallas import tpu as pltpu
from jax.sharding import PartitionSpec as P

learn_rate = 0.1
momentum_beta = 0.9
decay_keep = 0.999
epsilon = 1e-06

f32 = jnp.float32
bf16 = jnp.bfloat16
VMEM_LIMIT = 48 * 2**20


def ring_order(chips):
    if chips % 2:
        return list(range(chips))
    return list(range(0, chips, 2)) + list(range(chips - 1, 0, -2))


def ring_place(chips, chip):
    if chips % 2:
        return chip
    return jnp.where(chip % 2 == 0, chip // 2, chips - 1 - chip // 2)


def chip_at(chips, place):
    if chips % 2:
        return place
    return jnp.where(place < chips // 2, 2 * place, 2 * (chips - 1 - place) + 1)


class Ring:
    def __init__(self, devices):
        self.chips = devices // 2
        order = ring_order(self.chips)
        n = self.chips
        self.to_right = [
            (2 * order[p] + k, 2 * order[(p + 1) % n] + k) for p in range(n) for k in (0, 1)
        ]
        self.to_left = [(b, a) for a, b in self.to_right]
        self.pair = [(i, i ^ 1) for i in range(devices)]

    def right(self, x):
        return lax.ppermute(x, "fsdp", self.to_right)

    def left(self, x):
        return lax.ppermute(x, "fsdp", self.to_left)

    def swap(self, x):
        return lax.ppermute(x, "fsdp", self.pair)

    def hops(self, half):
        n = self.chips
        short = (n - 1) // 2
        long = n - 1 - short
        return (long, short) if half == 0 else (short, long)

    def gather(self, halves):
        n = self.chips
        slots = [[None] * n for _ in halves]
        moving = []
        for h, x in enumerate(halves):
            slots[h][0] = x
            moving.append([x, x])
        for s in range(1, n // 2 + 1):
            for h in range(len(halves)):
                to_right, to_left = self.hops(h)
                if s <= to_right:
                    moving[h][0] = self.right(moving[h][0])
                    slots[h][n - s] = moving[h][0]
                if s <= to_left:
                    moving[h][1] = self.left(moving[h][1])
                    slots[h][s] = moving[h][1]
        return slots

    def scatter_sum(self, slots):
        n = self.chips
        totals = []
        moving = [[None, None] for _ in slots]
        for s in range(n // 2, 0, -1):
            for h in range(len(slots)):
                to_right, to_left = self.hops(h)
                if s <= to_right:
                    term = slots[h][s]
                    if moving[h][0] is not None:
                        term = add_low(moving[h][0], term)
                    moving[h][0] = self.right(term)
                if s <= to_left:
                    term = slots[h][n - s]
                    if moving[h][1] is not None:
                        term = add_low(moving[h][1], term)
                    moving[h][1] = self.left(term)
        for h in range(len(slots)):
            total = slots[h][0].astype(f32)
            for part in moving[h]:
                if part is not None:
                    total = total + part.astype(f32)
            totals.append(total)
        return totals


def add_low(a, b):
    return (a.astype(f32) + b.astype(f32)).astype(bf16)


def forward_kernel(
    per_col, scaling, half_steps, n, scal, act_own, act_sib, *refs
):
    slots_a, slots_b = refs[:n], refs[n : 2 * n]
    res_own, res_sib, up_own, up_sib, gain = refs[2 * n : 2 * n + 5]
    pre, stats = refs[2 * n + 5 : 2 * n + 7]
    weight, sums = refs[2 * n + 7 :]
    step = pl.program_id(0)
    cols, block = slots_a[0].shape[0], slots_a[0].shape[3]
    depth = n * slots_a[0].shape[2]

    @pl.when(step == 0)
    def _():
        sums[...] = jnp.zeros_like(sums)

    def place(slots):
        for r in range(n):
            weight[scal[1 + r]] = slots[r][...]

    @pl.when(step < half_steps)
    def _():
        place(slots_a)

    @pl.when(step >= half_steps)
    def _():
        place(slots_b)

    for j in range(cols):
        at = 1 + n + (step * cols + j) * per_col
        lanes = [pl.ds(pl.multiple_of(scal[at + k] * block, block), block) for k in range(per_col)]
        w = jnp.concatenate(
            [weight[:, j, k].reshape(depth, block) for k in range(per_col)], axis=0
        )
        cut = slice(j * block, (j + 1) * block)
        for t, (act, res, up) in enumerate(((act_own, res_own, up_own), (act_sib, res_sib, up_sib))):
            x = jnp.concatenate([act[0, :, lane] for lane in lanes], axis=1)
            proj = jnp.dot(x, w, preferred_element_type=f32)
            value = res[0, :, cut].astype(f32) + scaling * proj
            pre[t, :, cut] = value
            g = gain[j] * up[0, :, cut].astype(f32)
            sums[t, 0] += value * value
            sums[t, 1] += value * g

    @pl.when(step == pl.num_programs(0) - 1)
    def _():
        lane = lax.broadcasted_iota(jnp.int32, stats.shape[1:], 1)
        for t in range(2):
            square = jnp.sum(sums[t, 0], axis=1, keepdims=True)
            inner = jnp.sum(sums[t, 1], axis=1, keepdims=True)
            stats[t] = jnp.where(lane < block // 2, square, inner)


def backward_kernel(
    per_col, width, half_steps, n, scal, act_t, pre, up_own, up_sib, gain, own, other, *refs
):
    out_a, out_b = refs[:n], refs[n : 2 * n]
    scales, grad, terms = refs[2 * n :]
    step = pl.program_id(0)
    cols, block = out_a[0].shape[0], out_a[0].shape[3]
    rows = pre.shape[1]
    depth = n * out_a[0].shape[2]

    @pl.when(step == 0)
    def _():
        grad[...] = jnp.zeros_like(grad)
        for t in range(2):
            total = own[t] + other[1 - t]
            square, inner = total[:, 0:1], total[:, block // 2 : block // 2 + 1]
            inv = lax.rsqrt(square / width + epsilon)
            scales[t, 0] = jnp.broadcast_to(inv, scales.shape[2:])
            scales[t, 1] = jnp.broadcast_to(inv * inv * inv * (inner / width), scales.shape[2:])

    for j in range(cols):
        at = 1 + n + (step * cols + j) * per_col
        cut = slice(j * block, (j + 1) * block)
        for t, up in enumerate((up_own, up_sib)):
            g = gain[j] * up[0, :, cut].astype(f32)
            value = scales[t, 0] * g - pre[t, :, cut] * scales[t, 1]
            grad[t * rows : (t + 1) * rows] = value.astype(bf16)
        x = jnp.concatenate([act_t[scal[at + k]] for k in range(per_col)], axis=0)
        term = jnp.dot(x, grad[...], preferred_element_type=f32).astype(bf16)
        terms[j] = term.reshape(per_col, n, depth // n, block)

    def place(outs):
        for r in range(n):
            outs[r][...] = terms[:, :, scal[1 + r]]

    @pl.when(step < half_steps)
    def _():
        place(out_a)

    @pl.when(step >= half_steps)
    def _():
        place(out_b)


def step_columns(columns):
    half = columns // 2
    return max(c for c in range(1, 6) if half % c == 0)


def forward(scal, step_num, activations, act_sib, slots, residual, res_sib, upstream, up_sib, gain, scaling):
    n = len(slots[0])
    half_cols, per_col, rows_in, block = slots[0][0].shape
    columns = 2 * half_cols
    cols = step_columns(columns)
    half_steps = half_cols // cols
    grid = columns // cols
    rows, features = activations.shape[1:]
    wide = cols * block

    whole = lambda: pl.BlockSpec((1, rows, features), lambda i, s: (step_num, 0, 0))
    first = lambda: pl.BlockSpec(
        (cols, per_col, rows_in, block), lambda i, s: (jnp.minimum(i, half_steps - 1), 0, 0, 0)
    )
    second = lambda: pl.BlockSpec(
        (cols, per_col, rows_in, block), lambda i, s: (jnp.maximum(i - half_steps, 0), 0, 0, 0)
    )
    mine = lambda: pl.BlockSpec((1, rows, wide), lambda i, s: (step_num, 0, s[0] * grid + i))
    theirs = lambda: pl.BlockSpec((1, rows, wide), lambda i, s: (step_num, 0, i))
    flops = 4 * rows * columns * per_col * block * block
    return pl.pallas_call(
        partial(forward_kernel, per_col, scaling, half_steps, n),
        grid_spec=pltpu.PrefetchScalarGridSpec(
            num_scalar_prefetch=1,
            grid=(grid,),
            in_specs=[whole(), whole()]
            + [first() for _ in range(n)]
            + [second() for _ in range(n)]
            + [mine(), theirs(), mine(), theirs()]
            + [pl.BlockSpec((cols, 1, block), lambda i, s: (i, 0, 0))],
            out_specs=[
                pl.BlockSpec((2, rows, wide), lambda i, s: (0, 0, i)),
                pl.BlockSpec((2, rows, block), lambda i, s: (0, 0, 0)),
            ],
            scratch_shapes=[
                pltpu.VMEM((n, cols, per_col, rows_in, block), bf16),
                pltpu.VMEM((2, 2, rows, block), f32),
            ],
        ),
        out_shape=[
            jax.ShapeDtypeStruct((2, rows, columns * block), f32),
            jax.ShapeDtypeStruct((2, rows, block), f32),
        ],
        compiler_params=pltpu.CompilerParams(vmem_limit_bytes=VMEM_LIMIT),
        cost_estimate=pl.CostEstimate(flops=flops, bytes_accessed=16 * 2**20, transcendentals=0),
        name="forward",
    )(scal, activations, act_sib, *slots[0], *slots[1], residual, res_sib, upstream, up_sib, gain)


def backward(scal, step_num, act_t, pre, upstream, up_sib, gain, own, other, shard, width):
    half_cols, per_col, rows_in, block = shard
    n = block // rows_in
    columns = 2 * half_cols
    cols = step_columns(columns)
    half_steps = half_cols // cols
    grid = columns // cols
    rows = pre.shape[1]
    wide = cols * block
    in_blocks, _, tokens = act_t.shape

    first = lambda: pl.BlockSpec(
        (cols, per_col, rows_in, block), lambda i, s: (jnp.minimum(i, half_steps - 1), 0, 0, 0)
    )
    second = lambda: pl.BlockSpec(
        (cols, per_col, rows_in, block), lambda i, s: (jnp.maximum(i - half_steps, 0), 0, 0, 0)
    )
    sums = lambda: pl.BlockSpec((2, rows, block), lambda i, s: (0, 0, 0))
    flops = 4 * rows * columns * per_col * block * block
    out = pl.pallas_call(
        partial(backward_kernel, per_col, width, half_steps, n),
        grid_spec=pltpu.PrefetchScalarGridSpec(
            num_scalar_prefetch=1,
            grid=(grid,),
            in_specs=[
                pl.BlockSpec((in_blocks, block, tokens), lambda i, s: (0, 0, 0)),
                pl.BlockSpec((2, rows, wide), lambda i, s: (0, 0, i)),
                pl.BlockSpec((1, rows, wide), lambda i, s: (step_num, 0, s[0] * grid + i)),
                pl.BlockSpec((1, rows, wide), lambda i, s: (step_num, 0, i)),
                pl.BlockSpec((cols, 1, block), lambda i, s: (i, 0, 0)),
                sums(),
                sums(),
            ],
            out_specs=[first() for _ in range(n)] + [second() for _ in range(n)],
            scratch_shapes=[
                pltpu.VMEM((2, 2, rows, block), f32),
                pltpu.VMEM((tokens, block), bf16),
                pltpu.VMEM((cols, per_col, n, rows_in, block), bf16),
            ],
        ),
        out_shape=[jax.ShapeDtypeStruct(shard, bf16) for _ in range(2 * n)],
        compiler_params=pltpu.CompilerParams(vmem_limit_bytes=VMEM_LIMIT),
        cost_estimate=pl.CostEstimate(flops=flops, bytes_accessed=16 * 2**20, transcendentals=0),
        name="backward",
    )(scal, act_t, pre, upstream, up_sib, gain, own, other)
    return [out[:n], out[n:]]


def gossip_with(stride, halves):
    devices = lax.axis_size("rep")
    stride = stride % devices
    if stride == 0:
        return halves
    shift = [(i, (i + stride) % devices) for i in range(devices)]
    return [
        0.5 * (own + lax.ppermute(own.astype(bf16), "rep", shift).astype(f32)) for own in halves
    ]


def gossip(which, halves):
    return lax.switch(which, [partial(gossip_with, hop) for hop in (1, 2, 4)], halves)


def body(activations, residual, upstream, norm_gain, params, momentum, pattern, step_index):
    steps, rows, features = activations.shape[1:]
    width = residual.shape[3]
    own_rows, out_blocks, per_col, block = params.shape[1:]
    scaling = 1.0 / math.sqrt(per_col * block)
    ring = Ring(lax.axis_size("fsdp"))
    n = ring.chips
    columns = out_blocks // 2
    half_cols = columns // 2

    me = lax.axis_index("fsdp")
    core = me % 2
    place = ring_place(n, me // 2)
    slot_chip = chip_at(n, (place + jnp.arange(n, dtype=jnp.int32)) % n)
    mine = lax.dynamic_slice_in_dim(pattern, core * columns, columns, 0)
    scal = jnp.concatenate([core[None], slot_chip, mine.reshape(-1)]).astype(jnp.int32)

    def by_rows(first, second):
        return jnp.concatenate(
            [jnp.where(core == 0, first, second), jnp.where(core == 0, second, first)], axis=-2
        )

    def to_work(x):
        turned = x.transpose(1, 2, 0, 3)
        kept = lax.dynamic_slice_in_dim(turned, core * columns, columns, 0)
        given = ring.swap(lax.dynamic_slice_in_dim(turned, (1 - core) * columns, columns, 0))
        both = by_rows(kept, given)
        return [both[:half_cols], both[half_cols:]]

    def to_own(halves):
        x = jnp.concatenate(halves, axis=0)
        kept = lax.dynamic_slice_in_dim(x, core * own_rows, own_rows, 2)
        given = ring.swap(lax.dynamic_slice_in_dim(x, (1 - core) * own_rows, own_rows, 2))
        both = jnp.concatenate(
            [jnp.where(core == 0, kept, given), jnp.where(core == 0, given, kept)], axis=0
        )
        return both.transpose(2, 0, 1, 3)

    weights = to_work(params[0])
    low = [w.astype(bf16) for w in weights]
    moment = to_work(momentum[0])

    act, res, up = activations[0], residual[0], upstream[0]
    theirs = (1 - core) * (width // 2)
    act_sib = ring.swap(act)
    res_sib = ring.swap(lax.dynamic_slice_in_dim(res, theirs, width // 2, 2))
    up_sib = ring.swap(lax.dynamic_slice_in_dim(up, theirs, width // 2, 2))
    gain = lax.dynamic_slice_in_dim(norm_gain, core * (width // 2), width // 2, 0)
    gain = gain.reshape(columns, 1, block)
    pad = -(2 * rows) % block
    act_t = []
    for s in range(steps):
        tokens = jnp.concatenate([act[s], act_sib[s], jnp.zeros((pad, features), bf16)], axis=0)
        act_t.append(tokens.T.reshape(features // block, block, 2 * rows + pad))

    for s in range(steps):
        slots = ring.gather(low)
        pre, own = forward(scal, s, act, act_sib, slots, res, res_sib, up, up_sib, gain, scaling)
        other = ring.swap(own)
        terms = backward(
            scal, s, act_t[s], pre, up, up_sib, gain, own, other, low[0].shape, float(width)
        )
        which = (step_index[0] + s) % 3
        if s < steps - 1:
            gradient = [scaling * g for g in ring.scatter_sum(terms)]
            moment = [momentum_beta * m + g for m, g in zip(moment, gradient)]
            weights = [decay_keep * w - learn_rate * m for w, m in zip(weights, moment)]
            weights = gossip(which, weights)
            low = [w.astype(bf16) for w in weights]
    moment_base = to_own([momentum_beta * m for m in moment])
    weight_base = to_own(
        [decay_keep * w - learn_rate * momentum_beta * m for w, m in zip(weights, moment)]
    )
    gradient = scaling * to_own(ring.scatter_sum(terms))
    moment_out = moment_base + gradient
    weight_out = gossip(which, [weight_base - learn_rate * gradient])[0]
    return (weight_out[None], moment_out[None])


def solution(mesh):
    in_specs = (
        P("rep", None, "fsdp", None),
        P("rep", None, "fsdp", None),
        P("rep", None, "fsdp", None),
        P(),
        P("rep", "fsdp", None, None, None),
        P("rep", "fsdp", None, None, None),
        P(),
        P(),
    )
    out_specs = (P("rep", "fsdp", None, None, None), P("rep", "fsdp", None, None, None))
    return jax.shard_map(body, mesh=mesh, in_specs=in_specs, out_specs=out_specs, check_vma=False)
```

time: 413 us -> 230 us (0.56); the launches traced: 412 us -> 234 us
  waiting for transfers between devices: 265 us -> 83.4 us
  starting transfers between devices: 0.16 us -> 71.5 us
  matrix products: 51.2 us -> 0 us
  Pallas kernels: 0 us -> 32 us
  local copies, waits for them, and re-layouts: 61.5 us -> 34.2 us
  between operations: 14.7 us -> 1.82 us
  other arithmetic: 19 us -> 10.6 us
    reduce_scatter x2 -> x0, waiting for transfers between devices: 170 us -> none  [body(): lax.psum_scatter(partial_sum.astype(jnp.bfloat16), 'fsdp', scatter_dimens...]
    all_gather x2 -> x0, waiting for transfers between devices: 95.4 us -> none  [body(): gathered = lax.all_gather(low_weights, 'fsdp', axis=0, tiled=True)]
    ppermute x0 -> x68, waiting for transfers between devices: none -> 83.4 us  [the longest x28 42.3 us: right(): return lax.ppermute(x, 'fsdp', self.to_right)]
    ppermute x0 -> x68, starting transfers between devices: none -> 71.5 us  [the longest x28 44.5 us: right(): return lax.ppermute(x, 'fsdp', self.to_right)]
    dot_general x4 -> x0, matrix products: 51.2 us -> none  [the longest x2 30.3 us: body(): jnp.einsum('tcki,tco->icko', picked, grad_low, preferred_element_type=jnp...]
    pallas_call x0 -> x4, Pallas kernels: none -> 32 us  [the longest x2 16.9 us: forward(): pl.pallas_call(partial(forward_kernel, per_col, scaling, half_steps, n),...]
    convert_element_type x2 -> x0, local copies, waits for them, and re-layouts: 21.4 us -> none  [body(): partial_sum.astype(jnp.bfloat16)]
    gather x2 -> x0, local copies, waits for them, and re-layouts: 19.3 us -> none  [body(): picked = jnp.take(blocks, pattern, axis=1)]
  transfers between devices with their start and end apart: 4 -> 68, of which waited for: 4 -> 44; matrix products, arithmetic and copies ran while one was open for 10% -> 11% of each run, Pallas kernels for 0% -> 0%
where the time goes in v1:
time: 230 us; the launch traced here: 234 us
  waiting for transfers between devices  83.4 us (36%)
  starting transfers between devices  71.5 us (31%)
  local copies, waits for them, and re-layouts  34.2 us (15%)
  Pallas kernels  32 us (14%)
  other arithmetic  10.6 us (5%)
    ppermute x28, starting transfers between devices, right(): return lax.ppermute(x, 'fsdp', self.to_right)  44.5 us
    ppermute x28, waiting for transfers between devices, right(): return lax.ppermute(x, 'fsdp', self.to_right)  42.3 us
    ppermute x28, waiting for transfers between devices, left(): return lax.ppermute(x, 'fsdp', self.to_left)  30.5 us
    ppermute x28, starting transfers between devices, left(): return lax.ppermute(x, 'fsdp', self.to_left)  23.5 us
    pallas_call x2, Pallas kernels, forward(): pl.pallas_call(partial(forward_kernel, per_col, scaling, half_steps, n),...  16.9 us
    pallas_call x2, Pallas kernels, backward(): pl.pallas_call(partial(backward_kernel, per_col, width, half_steps, n), g...  15.1 us
    unnamed x69, local copies, waits for them, and re-layouts  13.9 us
    transpose x2, local copies, waits for them, and re-layouts, body(): act_t.append(tokens.T.reshape(features // block, block, 2 * rows + pad))  8.17 us
  transfers between devices with their start and end apart: 68, of which 44 were waited for; matrix products, arithmetic and copies ran while one was open for 11% of the time, Pallas kernels for 0%

profile of v1, /device:TPU:0, one launch (start us, length us, event | category | flops | bytes accessed | tf_op | source)
XLA Modules:
  0.0 233.5 jit_solution(18126269881595546999)
XLA Ops:
  0.7 2.9 %constant_dynamic-slice_fusion.1 = (f32[1,8,20,5,128]{4,2,3,1,0:T(8,128)}, f32[1,8,20,5,128]{4,2,3,1,0:T(8,128)}, f32[1,8,20,5,128]{4,2,3,1,0:T(8,128)S(1)}, f32[1,8,20,5,128]{4,2,3,1,0:T(8,128)S(1)}) fusion(f32[1,8,40,5,128]{4,2,3,1,0:T(8,128)} %param.19, s32[]{:T(128)S(6)} %select_n.119, s32[]{:T(128)S(6)} %select_n.121, f32[1,8,40,5,128]{4,2,3,1,0:T(8,128)} %param.18), kind=kLoop, calls=%fused_computation.102 | loop fusion | bytes 3276808 | tf_op jit(solution)/shard_map/dynamic-slice.5
  4.1 2.8 %dynamic-slice_bitcast_fusion = bf16[2,176,2560]{2,1,0:T(8,128)(2,1)} fusion(bf16[1,2,176,5120]{3,2,1,0:T(8,128)(2,1)} %param.16, s32[]{:T(128)S(6)} %select_n.126), kind=kLoop, calls=%fused_computation.22 | loop fusion | bytes 3604484 | tf_op jit(solution)/shard_map/dynamic_slice | solution.py:372
  8.2 3.0 %collective-permute-start.17 = (bf16[10,5,16,128]{3,2,1,0:T(8,128)(2,1)S(1)}, bf16[10,5,16,128]{3,2,1,0:T(8,128)(2,1)S(1)}, u32[]{:S(2)}, u32[]{:S(2)}) collective-permute-start(bf16[10,5,16,128]{3,2,1,0:T(8,128)(2,1)S(1)} %get-tuple-element.256.refs_8_), channel_id=1, source_target_pairs={{0,4},{1,5},{4,8},{5,9},{8,12},{9,13},{12,14},{13,15},{14,10},{15,... | collective-permute-start | bytes 614408 | tf_op jit(solution)/shard_map/ppermute | solution.py:51
  22.8 4.5 %collective-permute-done.18.refs_14_ = bf16[10,5,16,128]{3,2,1,0:T(8,128)(2,1)S(1)} collective-permute-done((bf16[10,5,16,128]{3,2,1,0:T(8,128)(2,1)S(1)}, bf16[10,5,16,128]{3,2,1,0:T(8,128)(2,1)S(1)}, u32[]{:S(2)}, u32[]{:S(2)}) %collective-permute-start.18) | collective-permute-done | bytes 204832 | tf_op jit(solution)/shard_map/ppermute | solution.py:51
  29.3 3.8 %collective-permute-done.10.refs_6_ = bf16[10,5,16,128]{3,2,1,0:T(8,128)(2,1)} collective-permute-done((bf16[10,5,16,128]{3,2,1,0:T(8,128)(2,1)S(1)}, bf16[10,5,16,128]{3,2,1,0:T(8,128)(2,1)}, u32[]{:S(2)}, u32[]{:S(2)}) %collective-permute-start.10) | collective-permute-done | bytes 204832 | tf_op jit(solution)/shard_map/ppermute | solution.py:51
  35.2 3.9 %collective-permute-done.19.refs_13_ = bf16[10,5,16,128]{3,2,1,0:T(8,128)(2,1)S(1)} collective-permute-done((bf16[10,5,16,128]{3,2,1,0:T(8,128)(2,1)S(1)}, bf16[10,5,16,128]{3,2,1,0:T(8,128)(2,1)S(1)}, u32[]{:S(2)}, u32[]{:S(2)}) %collective-permute-start.19) | collective-permute-done | bytes 204832 | tf_op jit(solution)/shard_map/ppermute | solution.py:51
  42.5 2.8 %slice_bitcast_fusion.2 = (bf16[176,2560]{1,0:T(8,128)(2,1)}, bf16[176,2560]{1,0:T(8,128)(2,1)}) fusion(bf16[1,2,176,2560]{3,2,1,0:T(8,128)(2,1)} %param.14), kind=kLoop, calls=%fused_computation.38 | loop fusion | bytes 3604480 | tf_op jit(solution)/shard_map/squeeze | solution.py:378
  57.7 8.5 %forward.2 = (f32[2,176,2560]{2,1,0:T(8,128)}, f32[2,176,128]{2,1,0:T(8,128)}) custom-call(s32[109]{0:T(128)S(1)} %pad_add_fusion.scal, bf16[2,176,2560]{2,1,0:T(8,128)(2,1)} %bitcast.6.act_own, bf16[2,176,2560]{2,1,0:T(8,128)(2,1)} %collective-permute-done.3.act_sib, bf16[10,5,16,128]{3,2,1,0:T(8,128)(2,1)S(1)} %get-tuple-element.286.refs_0_, ...), custom_call_target="tpu_custom_call" | custom-call | flops 1153433600 | bytes 16777216 | tf_op jit(solution)/shard_map/forward/pallas_call | solution.py:234
  68.2 2.8 %maximum_bitcast_fusion.1 = (bf16[2560,384]{0,1:T(8,128)(2,1)}, bf16[2560,384]{0,1:T(8,128)(2,1)}) fusion(bf16[176,2560]{1,0:T(8,128)(2,1)S(1)} %get-tuple-element.270, bf16[176,2560]{1,0:T(8,128)(2,1)S(1)} %copy-done.24, bf16[384]{0:T(512)(128)(2,1)S(1)} %pad.21.clone, bf16[176,2560]{1,0:T(8,128)(2,1)S(1)} %get-tuple-element.271, ...), kind=kLoop, calls=%fused_computation.21 | loop fusion | flops 10813440 | bytes 7537408 | tf_op jit(solution)/shard_map/transpose | solution.py:379
  71.0 4.1 %copy.46 = bf16[2560,384]{1,0:T(8,128)(2,1)} copy(bf16[2560,384]{0,1:T(8,128)(2,1)} %get-tuple-element.290) | data formatting | bytes 3932160 | tf_op jit(solution)/shard_map/transpose | solution.py:379
  76.8 7.9 %backward.2 = (bf16[10,5,16,128]{3,2,1,0:T(8,128)(2,1)S(1)}, bf16[10,5,16,128]{3,2,1,0:T(8,128)(2,1)S(1)}, bf16[10,5,16,128]{3,2,1,0:T(8,128)(2,1)S(1)}, bf16[10...) custom-call(s32[109]{0:T(128)S(1)} %pad_add_fusion.scal, ...), custom_call_target="tpu_custom_call" | custom-call | flops 1153433600 | bytes 16777216 | tf_op jit(solution)/shard_map/backward/pallas_call | solution.py:282
  94.4 3.2 %collective-permute-done.23 = bf16[10,5,16,128]{3,2,1,0:T(8,128)(2,1)S(1)} collective-permute-done((bf16[10,5,16,128]{3,2,1,0:T(8,128)(2,1)}, bf16[10,5,16,128]{3,2,1,0:T(8,128)(2,1)S(1)}, u32[]{:S(2)}, u32[]{:S(2)}) %collective-permute-start.23) | collective-permute-done | bytes 204832 | tf_op jit(solution)/shard_map/ppermute | solution.py:51
  116.9 4.4 %collective-permute-done.35 = bf16[10,5,16,128]{3,2,1,0:T(8,128)(2,1)S(1)} collective-permute-done((bf16[10,5,16,128]{3,2,1,0:T(8,128)(2,1)S(1)}, bf16[10,5,16,128]{3,2,1,0:T(8,128)(2,1)S(1)}, u32[]{:S(2)}, u32[]{:S(2)}) %collective-permute-start.35) | collective-permute-done | bytes 204832 | tf_op jit(solution)/shard_map/ppermute | solution.py:54
  123.2 4.5 %collective-permute-done.36 = bf16[10,5,16,128]{3,2,1,0:T(8,128)(2,1)S(1)} collective-permute-done((bf16[10,5,16,128]{3,2,1,0:T(8,128)(2,1)S(1)}, bf16[10,5,16,128]{3,2,1,0:T(8,128)(2,1)S(1)}, u32[]{:S(2)}, u32[]{:S(2)}) %collective-permute-start.36) | collective-permute-done | bytes 204832 | tf_op jit(solution)/shard_map/ppermute | solution.py:54
  128.8 10.1 %conditional.5 = (f32[10,5,16,128]{3,2,1,0:T(8,128)S(1)}, f32[10,5,16,128]{3,2,1,0:T(8,128)S(1)}, bf16[10,5,16,128]{3,2,1,0:T(8,128)(2,1)S(1)}, bf16[10,5,16,128]{3,2,1,0:T(8,128)(2,1)S(1)}) conditional(s32[]{:T(128)} %clamp.7, (f32[10,5,16,128]{3,2,1,0:T(8,128)S(1)}, f32[10,5,16,128]{3,2,1,0:T(8,128)S(1)}, ...), branch_computations={%region_0.1_spmd, %region_1.2_spmd, %region_2.3_spmd} | conditional | flops 2252800 | bytes 7782512
  131.0 5.5 %collective-permute-done.2 = bf16[10,5,16,128]{3,2,1,0:T(8,128)(2,1)S(1)} collective-permute-done((bf16[10,5,16,128]{3,2,1,0:T(8,128)(2,1)S(1)}, bf16[10,5,16,128]{3,2,1,0:T(8,128)(2,1)S(1)}, u32[]{:S(2)}, u32[]{:S(2)}) %collective-permute-start.2) | collective-permute-done | bytes 204832 | tf_op jit(solution)/shard_map/cond/branch_0_fun/ppermute | solution.py:318
  144.0 3.6 %collective-permute-done.44.refs_9_ = bf16[10,5,16,128]{3,2,1,0:T(8,128)(2,1)S(1)} collective-permute-done((bf16[10,5,16,128]{3,2,1,0:T(8,128)(2,1)S(1)}, bf16[10,5,16,128]{3,2,1,0:T(8,128)(2,1)S(1)}, u32[]{:S(2)}, u32[]{:S(2)}) %collective-permute-start.44) | collective-permute-done | bytes 204832 | tf_op jit(solution)/shard_map/ppermute | solution.py:54
  150.0 2.8 %collective-permute-done.48.refs_15_ = bf16[10,5,16,128]{3,2,1,0:T(8,128)(2,1)S(1)} collective-permute-done((bf16[10,5,16,128]{3,2,1,0:T(8,128)(2,1)S(1)}, bf16[10,5,16,128]{3,2,1,0:T(8,128)(2,1)S(1)}, u32[]{:S(2)}, u32[]{:S(2)}) %collective-permute-start.48) | collective-permute-done | bytes 204832 | tf_op jit(solution)/shard_map/ppermute | solution.py:51
  158.6 4.0 %copy.41 = bf16[2560,384]{1,0:T(8,128)(2,1)} copy(bf16[2560,384]{0,1:T(8,128)(2,1)} %get-tuple-element.291) | data formatting | bytes 3932160 | tf_op jit(solution)/shard_map/transpose | solution.py:379
  172.3 8.4 %forward.3 = (f32[2,176,2560]{2,1,0:T(8,128)}, f32[2,176,128]{2,1,0:T(8,128)S(1)}) custom-call(s32[109]{0:T(128)S(1)} %pad_add_fusion.scal, bf16[2,176,2560]{2,1,0:T(8,128)(2,1)} %bitcast.6.act_own, bf16[2,176,2560]{2,1,0:T(8,128)(2,1)} %collective-permute-done.3.act_sib, bf16[10,5,16,128]{3,2,1,0:T(8,128)(2,1)} %copy-done.31, ...), custom_call_target="tpu_custom_call" | custom-call | flops 1153433600 | bytes 16777216 | tf_op jit(solution)/shard_map/forward/pallas_call | solution.py:234
  182.1 7.2 %backward.3 = (bf16[10,5,16,128]{3,2,1,0:T(8,128)(2,1)S(1)}, bf16[10,5,16,128]{3,2,1,0:T(8,128)(2,1)S(1)}, bf16[10,5,16,128]{3,2,1,0:T(8,128)(2,1)S(1)}, bf16[10...) custom-call(s32[109]{0:T(128)S(1)} %pad_add_fusion.scal, ...), custom_call_target="tpu_custom_call" | custom-call | flops 1153433600 | bytes 16777216 | tf_op jit(solution)/shard_map/backward/pallas_call | solution.py:282
  193.6 3.7 %collective-permute-done.52 = bf16[10,5,16,128]{3,2,1,0:T(8,128)(2,1)S(1)} collective-permute-done((bf16[10,5,16,128]{3,2,1,0:T(8,128)(2,1)S(1)}, bf16[10,5,16,128]{3,2,1,0:T(8,128)(2,1)S(1)}, u32[]{:S(2)}, u32[]{:S(2)}) %collective-permute-start.52) | collective-permute-done | bytes 204832 | tf_op jit(solution)/shard_map/ppermute | solution.py:51
  218.3 3.6 %collective-permute-done.64 = bf16[10,5,16,128]{3,2,1,0:T(8,128)(2,1)S(1)} collective-permute-done((bf16[10,5,16,128]{3,2,1,0:T(8,128)(2,1)S(1)}, bf16[10,5,16,128]{3,2,1,0:T(8,128)(2,1)S(1)}, u32[]{:S(2)}, u32[]{:S(2)}) %collective-permute-start.64) | collective-permute-done | bytes 204832 | tf_op jit(solution)/shard_map/ppermute | solution.py:54
  225.2 3.6 %collective-permute-done.55 = bf16[10,5,16,128]{3,2,1,0:T(8,128)(2,1)S(1)} collective-permute-done((bf16[10,5,16,128]{3,2,1,0:T(8,128)(2,1)S(1)}, bf16[10,5,16,128]{3,2,1,0:T(8,128)(2,1)S(1)}, u32[]{:S(2)}, u32[]{:S(2)}) %collective-permute-start.55) | collective-permute-done | bytes 204832 | tf_op jit(solution)/shard_map/ppermute | solution.py:51
  (247 shorter events, 130.5 us)
Async XLA Ops:
  7.0 47.6 %collective-permute-start.21 = (bf16[2,176,2560]{2,1,0:T(8,128)(2,1)}, bf16[2,176,2560]{2,1,0:T(8,128)(2,1)S(1)}, u32[]{:S(2)}, u32[]{:S(2)}) collective-permute-start(bf16[2,176,2560]{2,1,0:T(8,128)(2,1)} %dynamic-slice_bitcast_fusion), channel_id=1, source_target_pairs={{0,1},{1,0},{2,3},{3,2},{4,5},{5,4},{6,7},{7,6},{8,9},{9,8},{10,11... | collective-permute-start | bytes 5406728 | tf_op jit(solution)/shard_map/ppermute | solution.py:57
  8.2 8.8 %collective-permute-start.17 = (bf16[10,5,16,128]{3,2,1,0:T(8,128)(2,1)S(1)}, bf16[10,5,16,128]{3,2,1,0:T(8,128)(2,1)S(1)}, u32[]{:S(2)}, u32[]{:S(2)}) collective-permute-start(bf16[10,5,16,128]{3,2,1,0:T(8,128)(2,1)S(1)} %get-tuple-element.256.refs_8_), channel_id=1, source_target_pairs={{0,4},{1,5},{4,8},{5,9},{8,12},{9,13},{12,14},{13,15},{14,10},{15,... | collective-permute-start | bytes 614408 | tf_op jit(solution)/shard_map/ppermute | solution.py:51
  11.2 9.6 %collective-permute-start.9 = (bf16[10,5,16,128]{3,2,1,0:T(8,128)(2,1)S(1)}, bf16[10,5,16,128]{3,2,1,0:T(8,128)(2,1)S(1)}, u32[]{:S(2)}, u32[]{:S(2)}) collective-permute-start(bf16[10,5,16,128]{3,2,1,0:T(8,128)(2,1)S(1)} %get-tuple-element.286.refs_0_), channel_id=1, source_target_pairs={{0,4},{1,5},{4,8},{5,9},{8,12},{9,13},{12,14},{13,15},{14,10},{15,... | collective-permute-start | bytes 614408 | tf_op jit(solution)/shard_map/ppermute | solution.py:51
  13.2 9.4 %collective-permute-start.6 = (bf16[10,5,16,128]{3,2,1,0:T(8,128)(2,1)S(1)}, bf16[10,5,16,128]{3,2,1,0:T(8,128)(2,1)S(1)}, u32[]{:S(2)}, u32[]{:S(2)}) collective-permute-start(bf16[10,5,16,128]{3,2,1,0:T(8,128)(2,1)S(1)} %get-tuple-element.286.refs_0_), channel_id=1, source_target_pairs={{4,0},{5,1},{8,4},{9,5},{12,8},{13,9},{14,12},{15,13},{10,14},{11,... | collective-permute-start | bytes 614408 | tf_op jit(solution)/shard_map/ppermute | solution.py:54
  17.0 37.6 %collective-permute-start.20 = (bf16[2,176,2560]{2,1,0:T(8,128)(2,1)}, bf16[2,176,2560]{2,1,0:T(8,128)(2,1)}, u32[]{:S(2)}, u32[]{:S(2)}) collective-permute-start(bf16[2,176,2560]{2,1,0:T(8,128)(2,1)} %dynamic-slice_bitcast_fusion.1), channel_id=1, source_target_pairs={{0,1},{1,0},{2,3},{3,2},{4,5},{5,4},{6,7},{7,6},{8,9},{9,8},{10,11... | collective-permute-start | bytes 5406728 | tf_op jit(solution)/shard_map/ppermute | solution.py:57
  19.2 35.5 %collective-permute-start.3 = (bf16[2,176,2560]{2,1,0:T(8,128)(2,1)}, bf16[2,176,2560]{2,1,0:T(8,128)(2,1)}, u32[]{:S(2)}, u32[]{:S(2)}) collective-permute-start(bf16[2,176,2560]{2,1,0:T(8,128)(2,1)} %bitcast.6.act_own), channel_id=1, source_target_pairs={{0,1},{1,0},{2,3},{3,2},{4,5},{5,4},{6,7},{7,6},{8,9},{9,8},{10,11... | collective-permute-start | bytes 5406728 | tf_op jit(solution)/shard_map/ppermute | solution.py:57
  66.2 9.0 %collective-permute-start.22 = (f32[2,176,128]{2,1,0:T(8,128)}, f32[2,176,128]{2,1,0:T(8,128)S(1)}, u32[]{:S(2)}, u32[]{:S(2)}) collective-permute-start(f32[2,176,128]{2,1,0:T(8,128)} %get-tuple-element.169.own), channel_id=1, source_target_pairs={{0,1},{1,0},{2,3},{3,2},{4,5},{5,4},{6,7},{7,6},{8,9},{9,8},{10,11... | collective-permute-start | bytes 540680 | tf_op jit(solution)/shard_map/ppermute | solution.py:57
  90.9 31.2 %collective-permute-start.5 = (f32[20,5,8,128]{3,2,1,0:T(8,128)S(1)}, f32[20,5,8,128]{3,2,1,0:T(8,128)S(1)}, u32[]{:S(2)}, u32[]{:S(2)}) collective-permute-start(f32[20,5,8,128]{3,2,1,0:T(8,128)S(1)} %bitcast.72), channel_id=1, source_target_pairs={{0,1},{1,0},{2,3},{3,2},{4,5},{5,4},{6,7},{7,6},{8,9},{9,8},{10,11... | collective-permute-start | bytes 1228808 | tf_op jit(solution)/shard_map/ppermute | solution.py:57
  92.4 9.6 %collective-permute-start.30 = (bf16[10,5,16,128]{3,2,1,0:T(8,128)(2,1)}, bf16[10,5,16,128]{3,2,1,0:T(8,128)(2,1)S(1)}, u32[]{:S(2)}, u32[]{:S(2)}) collective-permute-start(bf16[10,5,16,128]{3,2,1,0:T(8,128)(2,1)} %copy-done.18), channel_id=1, source_target_pairs={{0,4},{1,5},{4,8},{5,9},{8,12},{9,13},{12,14},{13,15},{14,10},{15,... | collective-permute-start | bytes 614408 | tf_op jit(solution)/shard_map/ppermute | solution.py:51
  93.7 10.4 %collective-permute-start.33 = (bf16[10,5,16,128]{3,2,1,0:T(8,128)(2,1)}, bf16[10,5,16,128]{3,2,1,0:T(8,128)(2,1)S(1)}, u32[]{:S(2)}, u32[]{:S(2)}) collective-permute-start(bf16[10,5,16,128]{3,2,1,0:T(8,128)(2,1)} %copy-done.17), channel_id=1, source_target_pairs={{4,0},{5,1},{8,4},{9,5},{12,8},{13,9},{14,12},{15,13},{10,14},{11,... | collective-permute-start | bytes 614408 | tf_op jit(solution)/shard_map/ppermute | solution.py:54
  102.0 9.0 %collective-permute-start.31 = (bf16[10,5,16,128]{3,2,1,0:T(8,128)(2,1)S(1)}, bf16[10,5,16,128]{3,2,1,0:T(8,128)(2,1)S(1)}, u32[]{:S(2)}, u32[]{:S(2)}) collective-permute-start(bf16[10,5,16,128]{3,2,1,0:T(8,128)(2,1)S(1)} %add_convert_fusion.14), channel_id=1, source_target_pairs={{0,4},{1,5},{4,8},{5,9},{8,12},{9,13},{12,14},{13,15},{14,10},{15,... | collective-permute-start | bytes 614408 | tf_op jit(solution)/shard_map/ppermute | solution.py:51
  104.2 9.2 %collective-permute-start.34 = (bf16[10,5,16,128]{3,2,1,0:T(8,128)(2,1)S(1)}, bf16[10,5,16,128]{3,2,1,0:T(8,128)(2,1)S(1)}, u32[]{:S(2)}, u32[]{:S(2)}) collective-permute-start(bf16[10,5,16,128]{3,2,1,0:T(8,128)(2,1)S(1)} %add_convert_fusion.12), channel_id=1, source_target_pairs={{4,0},{5,1},{8,4},{9,5},{12,8},{13,9},{14,12},{15,13},{10,14},{11,... | collective-permute-start | bytes 614408 | tf_op jit(solution)/shard_map/ppermute | solution.py:54
  109.1 13.1 %collective-permute-start.29 = (bf16[10,5,16,128]{3,2,1,0:T(8,128)(2,1)S(1)}, bf16[10,5,16,128]{3,2,1,0:T(8,128)(2,1)S(1)}, u32[]{:S(2)}, u32[]{:S(2)}) collective-permute-start(bf16[10,5,16,128]{3,2,1,0:T(8,128)(2,1)S(1)} %add_convert_fusion.15), channel_id=1, source_target_pairs={{4,0},{5,1},{8,4},{9,5},{12,8},{13,9},{14,12},{15,13},{10,14},{11,... | collective-permute-start | bytes 614408 | tf_op jit(solution)/shard_map/ppermute | solution.py:54
  111.1 11.1 %collective-permute-start.32 = (bf16[10,5,16,128]{3,2,1,0:T(8,128)(2,1)S(1)}, bf16[10,5,16,128]{3,2,1,0:T(8,128)(2,1)S(1)}, u32[]{:S(2)}, u32[]{:S(2)}) collective-permute-start(bf16[10,5,16,128]{3,2,1,0:T(8,128)(2,1)S(1)} %add_convert_fusion.13), channel_id=1, source_target_pairs={{0,4},{1,5},{4,8},{5,9},{8,12},{9,13},{12,14},{13,15},{14,10},{15,... | collective-permute-start | bytes 614408 | tf_op jit(solution)/shard_map/ppermute | solution.py:51
  142.0 10.8 %collective-permute-start.48 = (bf16[10,5,16,128]{3,2,1,0:T(8,128)(2,1)S(1)}, bf16[10,5,16,128]{3,2,1,0:T(8,128)(2,1)S(1)}, u32[]{:S(2)}, u32[]{:S(2)}) collective-permute-start(bf16[10,5,16,128]{3,2,1,0:T(8,128)(2,1)S(1)} %get-tuple-element.239.refs_8_), channel_id=1, source_target_pairs={{0,4},{1,5},{4,8},{5,9},{8,12},{9,13},{12,14},{13,15},{14,10},{15,... | collective-permute-start | bytes 614408 | tf_op jit(solution)/shard_map/ppermute | solution.py:51
  143.6 10.8 %collective-permute-start.37 = (bf16[10,5,16,128]{3,2,1,0:T(8,128)(2,1)S(1)}, bf16[10,5,16,128]{3,2,1,0:T(8,128)(2,1)S(1)}, u32[]{:S(2)}, u32[]{:S(2)}) collective-permute-start(bf16[10,5,16,128]{3,2,1,0:T(8,128)(2,1)S(1)} %get-tuple-element.238.refs_0_), channel_id=1, source_target_pairs={{4,0},{5,1},{8,4},{9,5},{12,8},{13,9},{14,12},{15,13},{10,14},{11,... | collective-permute-start | bytes 614408 | tf_op jit(solution)/shard_map/ppermute | solution.py:54
  147.6 8.8 %collective-permute-start.45 = (bf16[10,5,16,128]{3,2,1,0:T(8,128)(2,1)S(1)}, bf16[10,5,16,128]{3,2,1,0:T(8,128)(2,1)S(1)}, u32[]{:S(2)}, u32[]{:S(2)}) collective-permute-start(bf16[10,5,16,128]{3,2,1,0:T(8,128)(2,1)S(1)} %collective-permute-done.44.refs_9_), channel_id=1, source_target_pairs={{4,0},{5,1},{8,4},{9,5},{12,8},{13,9},{14,12},{15,13},{10,14},{11,... | collective-permute-start | bytes 614408 | tf_op jit(solution)/shard_map/ppermute | solution.py:54
  152.8 9.8 %collective-permute-start.49 = (bf16[10,5,16,128]{3,2,1,0:T(8,128)(2,1)S(1)}, bf16[10,5,16,128]{3,2,1,0:T(8,128)(2,1)S(1)}, u32[]{:S(2)}, u32[]{:S(2)}) collective-permute-start(bf16[10,5,16,128]{3,2,1,0:T(8,128)(2,1)S(1)} %collective-permute-done.48.refs_15_), channel_id=1, source_target_pairs={{0,4},{1,5},{4,8},{5,9},{8,12},{9,13},{12,14},{13,15},{14,10},{15,... | collective-permute-start | bytes 614408 | tf_op jit(solution)/shard_map/ppermute | solution.py:51
  154.4 10.0 %collective-permute-start.38 = (bf16[10,5,16,128]{3,2,1,0:T(8,128)(2,1)S(1)}, bf16[10,5,16,128]{3,2,1,0:T(8,128)(2,1)S(1)}, u32[]{:S(2)}, u32[]{:S(2)}) collective-permute-start(bf16[10,5,16,128]{3,2,1,0:T(8,128)(2,1)S(1)} %collective-permute-done.37.refs_1_), channel_id=1, source_target_pairs={{4,0},{5,1},{8,4},{9,5},{12,8},{13,9},{14,12},{15,13},{10,14},{11,... | collective-permute-start | bytes 614408 | tf_op jit(solution)/shard_map/ppermute | solution.py:54
  190.9 38.5 %collective-permute-start.68 = (f32[20,5,8,128]{3,2,1,0:T(8,128)S(1)}, f32[20,5,8,128]{3,2,1,0:T(8,128)S(1)}, u32[]{:S(2)}, u32[]{:S(2)}) collective-permute-start(f32[20,5,8,128]{3,2,1,0:T(8,128)S(1)} %fusion.11), channel_id=1, source_target_pairs={{0,1},{1,0},{2,3},{3,2},{4,5},{5,4},{6,7},{7,6},{8,9},{9,8},{10,11... | collective-permute-start | bytes 1228808 | tf_op jit(solution)/shard_map/ppermute | solution.py:57
  191.0 38.3 %collective-permute-start.67 = (f32[20,5,8,128]{3,2,1,0:T(8,128)S(1)}, f32[20,5,8,128]{3,2,1,0:T(8,128)S(1)}, u32[]{:S(2)}, u32[]{:S(2)}) collective-permute-start(f32[20,5,8,128]{3,2,1,0:T(8,128)S(1)} %fusion.13), channel_id=1, source_target_pairs={{0,1},{1,0},{2,3},{3,2},{4,5},{5,4},{6,7},{7,6},{8,9},{9,8},{10,11... | collective-permute-start | bytes 1228808 | tf_op jit(solution)/shard_map/ppermute | solution.py:57
  192.1 9.0 %collective-permute-start.59 = (bf16[10,5,16,128]{3,2,1,0:T(8,128)(2,1)S(1)}, bf16[10,5,16,128]{3,2,1,0:T(8,128)(2,1)S(1)}, u32[]{:S(2)}, u32[]{:S(2)}) collective-permute-start(bf16[10,5,16,128]{3,2,1,0:T(8,128)(2,1)S(1)} %get-tuple-element.199), channel_id=1, source_target_pairs={{0,4},{1,5},{4,8},{5,9},{8,12},{9,13},{12,14},{13,15},{14,10},{15,... | collective-permute-start | bytes 614408 | tf_op jit(solution)/shard_map/ppermute | solution.py:51
  210.7 12.6 %collective-permute-start.58 = (bf16[10,5,16,128]{3,2,1,0:T(8,128)(2,1)S(1)}, bf16[10,5,16,128]{3,2,1,0:T(8,128)(2,1)S(1)}, u32[]{:S(2)}, u32[]{:S(2)}) collective-permute-start(bf16[10,5,16,128]{3,2,1,0:T(8,128)(2,1)S(1)} %add_convert_fusion.5), channel_id=1, source_target_pairs={{4,0},{5,1},{8,4},{9,5},{12,8},{13,9},{14,12},{15,13},{10,14},{11,... | collective-permute-start | bytes 614408 | tf_op jit(solution)/shard_map/ppermute | solution.py:54
  212.9 16.0 %collective-permute-start.61 = (bf16[10,5,16,128]{3,2,1,0:T(8,128)(2,1)S(1)}, bf16[10,5,16,128]{3,2,1,0:T(8,128)(2,1)S(1)}, u32[]{:S(2)}, u32[]{:S(2)}) collective-permute-start(bf16[10,5,16,128]{3,2,1,0:T(8,128)(2,1)S(1)} %add_convert_fusion.3), channel_id=1, source_target_pairs={{0,4},{1,5},{4,8},{5,9},{8,12},{9,13},{12,14},{13,15},{14,10},{15,... | collective-permute-start | bytes 614408 | tf_op jit(solution)/shard_map/ppermute | solution.py:51
  (78 other events, 511.4 us)
